TPU v7x, 32 devices: a whole 2x2x4 slice. The times are simulated.
32 devices in a mesh: mol: 2 (over y), pair: 4 (over z), virt: 2 (over x), rep: 2 (over core).
Axes of the slice: x: 2, y: 2, z: 4, core: 2. Of those that a mesh axis runs over, the one named last changes fastest.
Arguments:
- amplitudes: bfloat16 [12, 32, 384, 384], P(('mol', 'rep'), None, 'pair', 'virt'), parts along dimension 0, may hold values from -6 to 6
- integrals: bfloat16 [64, 384, 32, 384], P('mol', 'virt', 'pair'), parts along dimension 0, may hold values from -0.15625 to 0.15625
- occ_irrep: int32 [32], replicated, may hold values from 0 to 7, as said below
- virt_irrep: int32 [384], replicated, may hold values from 0 to 7, as said below
Outputs:
- cycle_term: float32 [384, 12, 32, 384], P('virt', ('mol', 'rep'), 'pair'), parts along dimension 1
There are 2 independent parts, one for each index of `mol`. A program takes and returns all parts, laid end to end along the dimension named above; an argument that names none is the same for every part. Nothing has to cross between parts.
Inputs may be any that keep to these rules, and one draw needn't show every extreme that they name: `occ_irrep`: labels never fall along the orbitals, the first is 0 and the last is 7. `virt_irrep`: labels never fall along the orbitals, the first is 0 and the last is 7.
All inputs are finite; a program needn't handle non-finite values.
Results may differ from a plain program's by a relative error of at most 0.0003.
Values may be sent and summed in bfloat16 or wider, within the bound.
A program may use at most 192 MiB of HBM per device.

v0:
```python
import functools

import jax
import jax.numpy as jnp
from jax import lax
from jax.experimental import pallas as pl
from jax.experimental.pallas import tpu as pltpu
from jax.sharding import PartitionSpec as P

LANES = 128
VMEM_LIMIT = 56 * 1024 * 1024
SLABS = 3
MESH = pl.DeviceIdType.MESH


def dense(amplitudes, integrals, sym_i, sym_a, sym_c, sym_j, occ_irrep, virt_irrep):
    sym_amps = (
        sym_i[:, None, None, None]
        ^ occ_irrep[None, :, None, None]
        ^ sym_a[None, None, :, None]
        ^ sym_c[None, None, None, :]
    )
    masked_amps = jnp.where(sym_amps == 0, amplitudes, jnp.zeros_like(amplitudes))
    partial_value = jnp.einsum(
        "ikac,kcjb->aijb",
        lax.all_gather(masked_amps, "pair", axis=2, tiled=True),
        integrals,
        preferred_element_type=jnp.float32,
    )
    cycle_local = lax.psum_scatter(partial_value, "virt", scatter_dimension=0, tiled=True)
    virt_rows = lax.dynamic_slice_in_dim(
        virt_irrep, lax.axis_index("virt") * cycle_local.shape[0], cycle_local.shape[0]
    )
    full_mask = (
        virt_rows[:, None, None, None]
        ^ sym_i[None, :, None, None]
        ^ sym_j[None, None, :, None]
        ^ virt_irrep[None, None, None, :]
    )
    return jnp.where(full_mask == 0, cycle_local, jnp.zeros_like(cycle_local))


def cycle_kernel(
    pack,
    occ_ref,
    syms_ref,
    amps_row_ref,
    table_ref,
    row_ref,
    col_ref,
    fold_c_ref,
    fold_b_ref,
    unfold_c_ref,
    amps_ref,
    ints_ref,
    out_ref,
    small,
    ints,
    part,
    arrived,
    block,
    held,
    slab,
    slab_sem,
    send_sem,
    recv_sem,
    part_send_sem,
    part_recv_sem,
):
    pairs, occ_i, kks, virt_a, _ = small.shape
    occs, virts, occ_j, orbitals = ints_ref.shape
    width = unfold_c_ref.shape[1]
    per = pairs // 2
    slots = slab.shape[0]
    me = lax.axis_index("pair")
    side = lax.axis_index("virt")

    barrier = pltpu.get_barrier_semaphore()
    for d in range(1, pairs):
        pl.semaphore_signal(
            barrier, inc=1, device_id={"pair": lax.rem(me + d, pairs)}, device_id_type=MESH
        )
    pl.semaphore_signal(barrier, inc=1, device_id={"virt": 1 - side}, device_id_type=MESH)

    def fetch(k):
        at = lax.rem(k, slots)
        return pltpu.make_async_copy(ints_ref.at[k], slab.at[at], slab_sem.at[at])

    for k in range(slots - 1):
        fetch(k).start()
    pl.semaphore_wait(barrier, pairs)

    inner = jnp.logical_and(me > 0, me < pairs - 1)

    def hop(i, src, dst, sem):
        return pltpu.make_async_remote_copy(
            src_ref=small.at[src, i],
            dst_ref=small.at[src, i],
            send_sem=send_sem.at[i, sem],
            recv_sem=recv_sem.at[i, src],
            device_id={"pair": dst},
            device_id_type=MESH,
        )

    def forward_near(i):
        @pl.when(inner)
        def _():
            hop(i, me - 1, me + 1, 2).wait_recv()
            hop(i, me - 1, me + 1, 2).start()
            hop(i, me + 1, me - 1, 3).wait_recv()
            hop(i, me + 1, me - 1, 3).start()

    def far_hop(i):
        src = 6 - 3 * me
        return hop(i, src, 3 - src, 4)

    def forward_far(i):
        @pl.when(inner)
        def _():
            far_hop(i).wait_recv()
            far_hop(i).start()

    @pl.loop(0, occ_i)
    def _(i):
        @pl.loop(0, kks)
        def _(kk):
            total = None
            for h in range(pack):
                k = kk + h * kks
                keep = amps_row_ref[...] == syms_ref[i, k]
                value = jnp.where(keep, amps_ref[i, k].astype(jnp.float32), 0.0)
                term = jnp.dot(
                    value.astype(jnp.bfloat16), fold_c_ref[h], preferred_element_type=jnp.float32
                )
                total = term if total is None else total + term
            small[me, i, kk] = total.astype(jnp.bfloat16)

        @pl.when(me < pairs - 1)
        def _():
            hop(i, me, me + 1, 0).start()

        @pl.when(me > 0)
        def _():
            hop(i, me, me - 1, 1).start()

    lane = lax.broadcasted_iota(jnp.int32, (virts, LANES), 1)
    chunk = 32

    @pl.loop(0, occs)
    def _(k):
        @pl.when(k + slots - 1 < occs)
        def _():
            fetch(k + slots - 1).start()

        for i in range(occ_i):
            @pl.when(k == 3 + 8 * i)
            def _():
                forward_near(i)

        fetch(k).wait()
        at = lax.rem(k, slots)
        label = occ_ref[k]
        for start in range(0, virts, chunk):
            rows = pl.ds(start, chunk)
            keep = table_ref[rows] == label
            value = jnp.where(keep, slab[at, rows].astype(jnp.float32), 0.0)
            value = value.reshape(chunk * occ_j, orbitals).astype(jnp.bfloat16)
            held[pl.ds(start * occ_j, chunk * occ_j), :] = jnp.dot(
                value, fold_b_ref[...], preferred_element_type=jnp.float32
            )
        base = pl.multiple_of(lax.rem(k, kks) * width + (k // kks) * virts, 16)
        for group in range(occ_j // pack):
            value = held[pl.ds(group * pack, virts, stride=occ_j), :]
            for h in range(1, pack):
                other = held[pl.ds(group * pack + h, virts, stride=occ_j), :]
                value = jnp.where(lane < h * (LANES // pack), value, other)
            ints[pl.ds(base, virts), pl.ds(group * LANES, LANES)] = value.astype(jnp.bfloat16)

    def pass_on(i, q):
        return pltpu.make_async_remote_copy(
            src_ref=part.at[i, (1 - side) * per + q],
            dst_ref=arrived.at[i, q],
            send_sem=part_send_sem.at[i, q],
            recv_sem=part_recv_sem.at[i, q],
            device_id={"virt": 1 - side},
            device_id_type=MESH,
        )

    @pl.loop(0, occ_i * pairs)
    def _(t):
        far = t // occ_i
        i = lax.rem(t, occ_i)
        low = me < 2
        p = jnp.where(
            far == 0,
            me,
            jnp.where(
                far == 1,
                jnp.where(low, 1 - me, 5 - me),
                jnp.where(far == 2, jnp.where(low, 2, 1), jnp.where(low, 3, 0)),
            ),
        )
        q = lax.rem(p, per)

        @pl.when(far == 1)
        def _():
            forward_far(i)

        @pl.when(jnp.logical_and(p != me, jnp.logical_not(inner)))
        def _():
            hop(i, p, p, 0).wait_recv()

        for kk in range(kks):
            value = jnp.dot(
                small[p, i, kk], unfold_c_ref[...], preferred_element_type=jnp.float32
            )
            keep = row_ref[i, p] == col_ref[kk]
            block[:, pl.ds(kk * width, width)] = jnp.where(keep, value, 0.0).astype(jnp.bfloat16)
        part[i, p] = jnp.dot(block[...], ints[...], preferred_element_type=jnp.float32)

        @pl.when(p // per != side)
        def _():
            pass_on(i, q).start()

    for i in range(occ_i):
        for q in range(per):
            pass_on(i, q).wait()
            out_ref[i, pl.ds(q * virt_a, virt_a), :] = part[i, side * per + q] + arrived[i, q]
    for i in range(occ_i):
        @pl.when(me < pairs - 1)
        def _():
            hop(i, me, me + 1, 0).wait_send()

        @pl.when(me > 0)
        def _():
            hop(i, me, me - 1, 1).wait_send()

        @pl.when(inner)
        def _():
            hop(i, me - 1, me + 1, 2).wait_send()
            hop(i, me + 1, me - 1, 3).wait_send()
            far_hop(i).wait_send()


def unfold_kernel(pack, row_ref, col_ref, part_ref, unfold_ref, out_ref):
    occs = out_ref.shape[2]
    for group in range(occs // pack):
        value = part_ref[0, :, pl.ds(group * LANES, LANES)]
        high = value.astype(jnp.bfloat16)
        low = (value - high.astype(jnp.float32)).astype(jnp.bfloat16)
        both = jnp.concatenate([high, low], axis=1)
        for h in range(pack):
            j = group * pack + h
            full = jnp.dot(both, unfold_ref[h], preferred_element_type=jnp.float32)
            out_ref[:, 0, j, :] = jnp.where(row_ref[0] == col_ref[j], full, 0.0)


def params():
    return pltpu.CompilerParams(vmem_limit_bytes=VMEM_LIMIT)


def one_hot(slots, cap, count, dtype=jnp.bfloat16):
    lanes = lax.broadcasted_iota(jnp.int32, (count, 1, LANES), 2)
    shift = lax.broadcasted_iota(jnp.int32, (count, 1, 1), 0) * cap
    return (slots[None, :, None] + shift == lanes).astype(dtype)


def folded(cap, amplitudes, integrals, sym_i, sym_a, sym_c, sym_j, occ_irrep, virt_irrep):
    pack = LANES // cap
    occ_i, occs, virt_a, virt_c = amplitudes.shape
    occ_j, orbitals = integrals.shape[2:]
    kks = occs // pack
    pairs = orbitals // virt_a
    first = jnp.sum((virt_irrep[None, :] < virt_irrep[:, None]).astype(jnp.int32), axis=1)
    slot_b = jnp.arange(orbitals, dtype=jnp.int32) - first
    begin_c = lax.axis_index("virt") * virt_c
    first_c = lax.dynamic_slice_in_dim(first, begin_c, virt_c)
    slot_c = jnp.arange(virt_c, dtype=jnp.int32) + begin_c - jnp.maximum(first_c, begin_c)

    whole = lambda *dims: pl.BlockSpec(dims, lambda *_: (0,) * len(dims))
    smem = pl.BlockSpec(memory_space=pltpu.SMEM)
    fold_c = one_hot(slot_c, cap, pack)
    fold_b = one_hot(slot_b, cap, pack).sum(0).astype(jnp.bfloat16)
    width = pack * virt_c
    unfold_c = jnp.concatenate([fold_c[h].T for h in range(pack)], axis=1)
    cols = (occ_irrep.reshape(pack, kks).T[:, :, None] ^ sym_c[None, None, :]).reshape(kks, 1, width)
    rows = (sym_i[:, None] ^ virt_irrep[None, :])[:, :, None]
    vmem = pl.BlockSpec(memory_space=pltpu.VMEM)
    wide = occ_j * cap
    total = pl.pallas_call(
        functools.partial(cycle_kernel, pack),
        in_specs=[smem, smem] + [vmem] * 8 + [pl.BlockSpec(memory_space=pl.ANY)],
        out_specs=vmem,
        out_shape=jax.ShapeDtypeStruct((occ_i, orbitals // 2, wide), jnp.float32),
        scratch_shapes=[
            pltpu.VMEM((pairs, occ_i, kks, virt_a, LANES), jnp.bfloat16),
            pltpu.VMEM((kks * width, wide), jnp.bfloat16),
            pltpu.VMEM((occ_i, pairs, virt_a, wide), jnp.float32),
            pltpu.VMEM((occ_i, pairs // 2, virt_a, wide), jnp.float32),
            pltpu.VMEM((virt_a, kks * width), jnp.bfloat16),
            pltpu.VMEM((virt_c * occ_j, LANES), jnp.float32),
            pltpu.VMEM((SLABS, virt_c, occ_j, orbitals), jnp.bfloat16),
            pltpu.SemaphoreType.DMA((SLABS,)),
            pltpu.SemaphoreType.DMA((occ_i, 5)),
            pltpu.SemaphoreType.DMA((occ_i, pairs)),
            pltpu.SemaphoreType.DMA((occ_i, pairs // 2)),
            pltpu.SemaphoreType.DMA((occ_i, pairs // 2)),
        ],
        compiler_params=pltpu.CompilerParams(
            vmem_limit_bytes=VMEM_LIMIT, collective_id=pack, has_side_effects=True
        ),
        cost_estimate=pl.CostEstimate(
            flops=2 * integrals.size * 256, bytes_accessed=2 * integrals.size, transcendentals=0
        ),
        name="cycle",
    )(
        occ_irrep,
        sym_i[:, None] ^ occ_irrep[None, :],
        sym_a[:, None] ^ sym_c[None, :],
        sym_c[:, None, None] ^ sym_j[None, :, None] ^ virt_irrep[None, None, :],
        rows.reshape(occ_i, pairs, virt_a, 1),
        cols,
        fold_c,
        fold_b,
        unfold_c,
        amplitudes,
        integrals,
    )

    virt_v = total.shape[1]
    rows_v = lax.dynamic_slice_in_dim(rows, lax.axis_index("virt") * virt_v, virt_v, axis=1)
    cols_b = (sym_j[:, None] ^ virt_irrep[None, :])[:, None, :]
    unfold_b = one_hot(slot_b, cap, pack).transpose(0, 2, 1)
    unfold_b = jnp.concatenate([unfold_b, unfold_b], axis=1)
    return pl.pallas_call(
        functools.partial(unfold_kernel, pack),
        grid=(occ_i,),
        in_specs=[
            pl.BlockSpec((1, virt_v, 1), lambda i: (i, 0, 0)),
            whole(occ_j, 1, orbitals),
            pl.BlockSpec((1, virt_v, occ_j * cap), lambda i: (i, 0, 0)),
            whole(pack, 2 * LANES, orbitals),
        ],
        out_specs=pl.BlockSpec((virt_v, 1, occ_j, orbitals), lambda i: (0, i, 0, 0)),
        out_shape=jax.ShapeDtypeStruct((virt_v, occ_i, occ_j, orbitals), jnp.float32),
        compiler_params=params(),
        name="unfold",
    )(rows_v, cols_b, total, unfold_b)


def shards(mesh, amplitudes, integrals, occ_irrep, virt_irrep):
    occ_local, occs, virt_pair, virt_slice = amplitudes.shape
    occ_pair = integrals.shape[2]
    sym_i = lax.dynamic_slice_in_dim(occ_irrep, lax.axis_index("rep") * occ_local, occ_local)
    sym_a = lax.dynamic_slice_in_dim(virt_irrep, lax.axis_index("pair") * virt_pair, virt_pair)
    sym_c = lax.dynamic_slice_in_dim(virt_irrep, lax.axis_index("virt") * virt_slice, virt_slice)
    sym_j = lax.dynamic_slice_in_dim(occ_irrep, lax.axis_index("pair") * occ_pair, occ_pair)
    args = (amplitudes, integrals, sym_i, sym_a, sym_c, sym_j, occ_irrep, virt_irrep)
    fits = (
        mesh.shape["virt"] == 2
        and mesh.shape["pair"] == 4
        and occ_pair % 8 == 0
        and virt_pair % 32 == 0
        and virt_slice % 64 == 0
        and occs % 4 == 0
        and virt_irrep.shape[0] % LANES == 0
    )
    if not fits:
        return dense(*args)
    labels = jnp.arange(8, dtype=jnp.int32)
    largest = jnp.max(jnp.sum((virt_irrep[None, :] == labels[:, None]).astype(jnp.int32), axis=1))
    branch = (largest > 64).astype(jnp.int32) + (largest > 128).astype(jnp.int32)
    return lax.switch(
        branch, [functools.partial(folded, 64), functools.partial(folded, 128), dense], *args
    )


def solution(mesh):
    return jax.shard_map(
        functools.partial(shards, mesh),
        mesh=mesh,
        in_specs=(
            P(("mol", "rep"), None, "pair", "virt"),
            P("mol", "virt", "pair", None),
            P(),
            P(),
        ),
        out_specs=P("virt", ("mol", "rep"), "pair", None),
        check_vma=False,
    )
```

profile of v0, /device:TPU:0, one launch (start us, length us, event | category | flops | bytes accessed | tf_op | source)
XLA Modules:
  0.0 137.5 jit_solution(7980627105463080177)
XLA Ops:
  6.5 0.8 convert_reduce_fusion.2
  7.3 0.6 reduce_max.9
  9.3 0.7 dynamic_slice.27
  10.0 0.7 dynamic_slice.28
  10.7 0.8 dynamic_slice.29
  11.5 0.8 dynamic_slice.30
  12.2 115.5 %conditional.1 = (f32[192,3,8,384]{3,2,1,0:T(8,128)S(1)}) conditional(s32[]{:T(128)} %clamp.3, (s32[3]{0:T(128)S(1)}, s32[384]{0:T(512)}, s32[8]{0:T(128)S(1)}, s32[32]{0:T(128)}, s32[96]{0:T(128)S(1)}, /*index=5*/s32[192]{0:T(256)S(1)}, bf16[3,32,96,192]{3,2,1,0:T(8,128)(2,1)}, bf16[32,192,8,384]{3,2,1,0:T(8,128)(2,1)}) %tuple.14, ...), branch_computations={%region_2.0_spmd, %region_5.7_spmd, %region_7.9_spmd} | conditional | flops 43497172992 | bytes 224260608 | solution.py:373
  12.2 0.8 dynamic-slice.6
  13.1 0.9 copy.20.row_ref
  14.0 1.4 broadcast_xor_fusion.5.col_ref
  15.3 1.3 broadcast_xor_fusion.6.syms_ref
  16.6 0.7 broadcast_xor_fusion.3.amps_row_ref
  17.4 0.1 broadcast_xor_fusion.2
  17.5 2.4 %broadcast_xor_fusion.table_ref = s32[192,8,384]{2,1,0:T(8,128)} fusion(s32[384]{0:T(512)} %get-tuple-element.58, s32[192,8]{1,0:T(8,128)S(1)} %broadcast_xor_fusion.2), kind=kLoop, calls=%fused_computation | loop fusion | flops 589824 | bytes 2366976 | tf_op jit(solution)/shard_map/cond/branch_0_fun/xor | solution.py:320
  19.8 0.8 xor.295
  20.6 1.0 broadcast_xor_fusion.1.row_ref
  21.6 0.7 reshape.518
  22.3 0.1 copy.18
  22.4 0.1 xor.298
  22.5 0.1 xor.299
  22.6 0.1 xor.301
  22.7 0.6 broadcast_xor_fusion.4.col_ref
  23.3 1.0 convert_reduce_fusion
  24.3 0.1 maximum_subtract_fusion
  24.5 0.7 copy.19.fold_c_ref
  25.2 0.1 broadcast_add_fusion
  25.3 0.8 fusion.2.fold_b_ref
  26.1 0.7 pad_maximum_fusion.unfold_c_ref
  26.8 94.6 %cycle.2.part_ref = f32[3,192,512]{2,1,0:T(8,128)} custom-call(s32[32]{0:T(128)} %get-tuple-element.60.occ_ref, s32[3,32]{1,0:T(4,128)} %broadcast_xor_fusion.6.syms_ref, s32[96,192]{1,0:T(8,128)} %broadcast_xor_fusion.3.amps_row_ref, s32[192,8,384]{2,1,0:T(8,128)} %broadcast_xor_fusion.table_ref, s32[3,4,96,1]{3,2,1,0:T(8,128)} %broadcast_xor_fusion.1.row_ref, ...), custom_call_target="tpu_custom_call" | custom-call | flops 9663676416 | bytes 37748736 | tf_op jit(solution)/shard_map/cond/branch_0_fun/cycle/pallas_call | solution.py:290
  121.5 0.8 add_convert_fusion.unfold_ref
  122.3 5.2 %unfold.2 = f32[192,3,8,384]{3,2,1,0:T(8,128)S(1)} custom-call(s32[3,192,1]{2,1,0:T(8,128)} %copy.20.row_ref, s32[8,1,384]{2,1,0:T(1,128)} %broadcast_xor_fusion.5.col_ref, f32[3,192,512]{2,1,0:T(8,128)} %cycle.2.part_ref, bf16[2,256,384]{2,1,0:T(8,128)(2,1)} %add_convert_fusion.unfold_ref), custom_call_target="tpu_custom_call" | custom-call | tf_op jit(solution)/shard_map/cond/branch_0_fun/unfold/pallas_call | solution.py:335
  127.7 3.0 %copy-done = f32[192,3,8,384]{3,2,1,0:T(8,128)} copy-done((f32[192,3,8,384]{3,2,1,0:T(8,128)}, f32[192,3,8,384]{3,2,1,0:T(8,128)S(1)}, u32[]{:S(2)}) %copy-start) | copy-done | bytes 7077912
  (9 shorter events, 0.3 us)
Async XLA Ops:
  127.7 3.0 %copy-start = (f32[192,3,8,384]{3,2,1,0:T(8,128)}, f32[192,3,8,384]{3,2,1,0:T(8,128)S(1)}, u32[]{:S(2)}) copy-start(f32[192,3,8,384]{3,2,1,0:T(8,128)S(1)} %get-tuple-element.120) | copy-start | bytes 21233668
where the time goes:
time: 138 us
  Pallas kernels  99.8 us (72%)
  between operations  14.7 us (11%)
  other arithmetic  12.6 us (9%)
  local copies, waits for them, and re-layouts  10.2 us (7%)
    pallas_call x1, Pallas kernels, folded(): pl.pallas_call(functools.partial(cycle_kernel, pack), in_specs=[smem, sme...  94.6 us
    pallas_call x1, Pallas kernels, folded(): pl.pallas_call(functools.partial(unfold_kernel, pack), grid=(occ_i,), in_...  5.23 us
    unnamed x2, local copies, waits for them, and re-layouts  2.96 us

commit v1 on v0

--- a/solution.py
+++ b/solution.py
@@ -127,7 +127,7 @@
             total = None
             for h in range(pack):
                 k = kk + h * kks
-                keep = amps_row_ref[...] == syms_ref[i, k]
+                keep = amps_row_ref[...] == (syms_ref[i] ^ occ_ref[k])
                 value = jnp.where(keep, amps_ref[i, k].astype(jnp.float32), 0.0)
                 term = jnp.dot(
                     value.astype(jnp.bfloat16), fold_c_ref[h], preferred_element_type=jnp.float32
@@ -186,6 +186,8 @@
             device_id_type=MESH,
         )
 
+    place = lax.broadcasted_iota(jnp.int32, (1, width), 1)
+
     @pl.loop(0, occ_i * pairs)
     def _(t):
         far = t // occ_i
@@ -214,7 +216,10 @@
             value = jnp.dot(
                 small[p, i, kk], unfold_c_ref[...], preferred_element_type=jnp.float32
             )
-            keep = row_ref[i, p] == col_ref[kk]
+            label = occ_ref[kk]
+            for h in range(1, pack):
+                label = jnp.where(place < h * virts, label, occ_ref[kk + h * kks])
+            keep = row_ref[i, p] == (col_ref[...] ^ label)
             block[:, pl.ds(kk * width, width)] = jnp.where(keep, value, 0.0).astype(jnp.bfloat16)
         part[i, p] = jnp.dot(block[...], ints[...], preferred_element_type=jnp.float32)
 
@@ -283,7 +288,7 @@
     fold_b = one_hot(slot_b, cap, pack).sum(0).astype(jnp.bfloat16)
     width = pack * virt_c
     unfold_c = jnp.concatenate([fold_c[h].T for h in range(pack)], axis=1)
-    cols = (occ_irrep.reshape(pack, kks).T[:, :, None] ^ sym_c[None, None, :]).reshape(kks, 1, width)
+    cols = jnp.concatenate([sym_c] * pack)[None, :]
     rows = (sym_i[:, None] ^ virt_irrep[None, :])[:, :, None]
     vmem = pl.BlockSpec(memory_space=pltpu.VMEM)
     wide = occ_j * cap
@@ -315,7 +320,7 @@
         name="cycle",
     )(
         occ_irrep,
-        sym_i[:, None] ^ occ_irrep[None, :],
+        sym_i,
         sym_a[:, None] ^ sym_c[None, :],
         sym_c[:, None, None] ^ sym_j[None, :, None] ^ virt_irrep[None, None, :],
         rows.reshape(occ_i, pairs, virt_a, 1),

time: 138 us -> 136 us (0.986)
  other arithmetic: 12.6 us -> 10.7 us
    xor x2 -> x0, other arithmetic: 1.94 us -> none  [the longest x1 1.32 us: folded(): sym_i[:, None] ^ occ_irrep[None, :]]
where the time goes in v1:
time: 136 us; the launch traced here: 135 us
  Pallas kernels  99.8 us (73%)
  between operations  14.7 us (11%)
  other arithmetic  10.7 us (8%)
  local copies, waits for them, and re-layouts  9.65 us (7%)
    pallas_call x1, Pallas kernels, folded(): pl.pallas_call(functools.partial(cycle_kernel, pack), in_specs=[smem, sme...  94.5 us
    pallas_call x1, Pallas kernels, folded(): pl.pallas_call(functools.partial(unfold_kernel, pack), grid=(occ_i,), in_...  5.23 us
    unnamed x2, local copies, waits for them, and re-layouts  2.96 us

profile of v1, /device:TPU:0, one launch (start us, length us, event | category | flops | bytes accessed | tf_op | source)
XLA Modules:
  0.0 135.1 jit_solution(5185599022347515918)
XLA Ops:
  6.5 0.8 convert_reduce_fusion.2
  7.3 0.6 reduce_max.9
  9.3 0.7 dynamic_slice.27
  10.0 0.7 dynamic_slice.28
  10.7 0.8 dynamic_slice.29
  11.5 0.8 dynamic_slice.30
  12.2 113.1 %conditional.1 = (f32[192,3,8,384]{3,2,1,0:T(8,128)S(1)}) conditional(s32[]{:T(128)} %clamp.3, (s32[3]{0:T(128)S(1)}, s32[384]{0:T(512)}, s32[8]{0:T(128)S(1)}, s32[96]{0:T(128)S(1)}, s32[192]{0:T(256)S(1)}, /*index=5*/s32[32]{0:T(128)}, bf16[3,32,96,192]{3,2,1,0:T(8,128)(2,1)}, bf16[32,192,8,384]{3,2,1,0:T(8,128)(2,1)}) %tuple.14, ...), branch_computations={%region_2.0_spmd, %region_5.7_spmd, %region_7.9_spmd} | conditional | flops 43497172992 | bytes 224260608 | solution.py:378
  12.2 0.8 dynamic-slice.6
  13.0 0.1 xor_bitcast_fusion
  13.1 0.9 copy.17.row_ref
  14.0 1.4 %broadcast_xor_fusion.4.col_ref = s32[8,1,384]{2,1,0:T(1,128)} fusion(s32[384]{0:T(512)} %get-tuple-element.58, s32[8]{0:T(128)S(1)} %get-tuple-element.59), kind=kLoop, calls=%fused_computation.15 | loop fusion | flops 3072 | bytes 13856 | tf_op jit(solution)/shard_map/cond/branch_0_fun/xor | solution.py:337
  15.3 0.7 broadcast_xor_fusion.3.amps_row_ref
  16.0 0.1 broadcast_xor_fusion.2
  16.1 2.4 %broadcast_xor_fusion.table_ref = s32[192,8,384]{2,1,0:T(8,128)} fusion(s32[384]{0:T(512)} %get-tuple-element.58, s32[192,8]{1,0:T(8,128)S(1)} %broadcast_xor_fusion.2), kind=kLoop, calls=%fused_computation | loop fusion | flops 589824 | bytes 2366976 | tf_op jit(solution)/shard_map/cond/branch_0_fun/xor | solution.py:325
  18.5 0.8 xor.242
  19.3 1.0 broadcast_xor_fusion.1.row_ref
  20.2 0.1 pad_add_fusion
  20.3 0.6 broadcast_in_dim.0.col_ref
  20.9 1.0 convert_reduce_fusion
  21.9 0.1 maximum_subtract_fusion
  22.0 0.1 broadcast_add_fusion.1
  22.1 0.7 copy.16.fold_c_ref
  22.8 0.1 broadcast_add_fusion
  22.9 0.8 fusion.2.fold_b_ref
  23.7 0.7 pad_maximum_fusion.unfold_c_ref
  24.4 94.5 %cycle.2.part_ref = f32[3,192,512]{2,1,0:T(8,128)} custom-call(s32[32]{0:T(128)} %get-tuple-element.60.occ_ref, s32[3]{0:T(128)S(1)} %get-tuple-element.56.syms_ref, s32[96,192]{1,0:T(8,128)} %broadcast_xor_fusion.3.amps_row_ref, s32[192,8,384]{2,1,0:T(8,128)} %broadcast_xor_fusion.table_ref, s32[3,4,96,1]{3,2,1,0:T(8,128)} %broadcast_xor_fusion.1.row_ref, ...), custom_call_target="tpu_custom_call" | custom-call | flops 9663676416 | bytes 37748736 | tf_op jit(solution)/shard_map/cond/branch_0_fun/cycle/pallas_call | solution.py:295
  119.0 0.1 iota_compare_fusion
  119.1 0.8 add_convert_fusion.unfold_ref
  119.8 5.2 %unfold.2 = f32[192,3,8,384]{3,2,1,0:T(8,128)S(1)} custom-call(s32[3,192,1]{2,1,0:T(8,128)} %copy.17.row_ref, s32[8,1,384]{2,1,0:T(1,128)} %broadcast_xor_fusion.4.col_ref, f32[3,192,512]{2,1,0:T(8,128)} %cycle.2.part_ref, bf16[2,256,384]{2,1,0:T(8,128)(2,1)} %add_convert_fusion.unfold_ref), custom_call_target="tpu_custom_call" | custom-call | tf_op jit(solution)/shard_map/cond/branch_0_fun/unfold/pallas_call | solution.py:340
  125.3 0.0 copy-start
  125.3 3.0 %copy-done = f32[192,3,8,384]{3,2,1,0:T(8,128)} copy-done((f32[192,3,8,384]{3,2,1,0:T(8,128)}, f32[192,3,8,384]{3,2,1,0:T(8,128)S(1)}, u32[]{:S(2)}) %copy-start) | copy-done | bytes 7077912
  (4 shorter events, 0.0 us)
Async XLA Ops:
  125.3 3.0 %copy-start = (f32[192,3,8,384]{3,2,1,0:T(8,128)}, f32[192,3,8,384]{3,2,1,0:T(8,128)S(1)}, u32[]{:S(2)}) copy-start(f32[192,3,8,384]{3,2,1,0:T(8,128)S(1)} %get-tuple-element.120) | copy-start | bytes 21233668
